TPU v7x, 512 devices: a whole 4x8x8 slice. The times are simulated.
512 devices in a mesh: tm: 64 (over y, z), space: 8 (over x, core).
Axes of the slice: x: 4, y: 8, z: 8, core: 2. Of those that a mesh axis runs over, the one named last changes fastest.
Arguments:
- fields: bfloat16 [16384, 3, 12288], P('tm', None, 'space'), may hold values from -100 to 100
- test_matrix: bfloat16 [64, 3, 12288], P(None, None, 'space'), may hold values from -0.03125 to 0.03125
Outputs:
- pcs: float32 [64, 16384], P(None, 'tm')
- energy: float32 [3, 12288], P(None, 'space')
All inputs are finite; a program needn't handle non-finite values.
Results may differ from a plain program's by a relative error of at most 0.0035.
Values may be sent and summed in bfloat16 or wider, within the bound.
A program may use at most 64 MiB of HBM per device.

v0:
```python
import math

import jax
import jax.numpy as jnp
import numpy as np
from jax import lax
from jax.sharding import PartitionSpec as P

HALF = 100
ITERS = 2


low_cutoff = 1.0 / 96.0
high_cutoff = 1.0 / 24.0


def with_halo(array, sides, width):
    for axis, dim in sides:
        devices, length = (lax.axis_size(axis), array.shape[dim])
        up = [(i, (i + 1) % devices) for i in range(devices - 1)]
        down = [(j, i) for i, j in up]
        last = lax.slice_in_dim(array, length - width, length, axis=dim)
        first = lax.slice_in_dim(array, 0, width, axis=dim)
        before = lax.ppermute(last, axis, up)
        after = lax.ppermute(first, axis, down)
        array = jnp.concatenate([before, array, after], axis=dim)
    return array


def lanczos_band(row_count, half_width):
    lag_table = (
        np.arange(row_count + 2 * half_width)[None, :] - np.arange(row_count)[:, None] - half_width
    ) * 1.0
    safe_lag = np.where(lag_table == 0, 1.0, lag_table)
    response = (
        np.sin(2 * np.pi * high_cutoff * safe_lag) - np.sin(2 * np.pi * low_cutoff * safe_lag)
    ) / (np.pi * safe_lag)
    response = np.where(lag_table == 0, 2.0 * (high_cutoff - low_cutoff), response)
    ratio = np.pi * safe_lag / (half_width + 1)
    sigma_factor = np.where(lag_table == 0, 1.0, np.sin(ratio) / ratio)
    return np.where(np.abs(lag_table) <= half_width, response * sigma_factor, 0.0).astype(
        np.float32
    )


def orthonormal(partial_sketch):
    sketch = lax.psum(partial_sketch, "space")
    gram_local = jnp.dot(sketch, sketch.T, precision=lax.Precision.HIGHEST)
    gram_total = lax.psum(gram_local, "tm")
    lower_factor = jnp.linalg.cholesky(gram_total)
    return jax.scipy.linalg.solve_triangular(lower_factor, sketch, lower=True)


def body(fields, test_matrix):
    time_rows, field_count, columns = fields.shape
    flat_width = field_count * columns
    rank_total = test_matrix.shape[0]
    rank_rows = rank_total // lax.axis_size("tm")
    total_times = time_rows * lax.axis_size("tm")
    padded = with_halo(fields, (("tm", 0),), HALF)
    filter_band = jnp.asarray(lanczos_band(time_rows, HALF)).astype(jnp.bfloat16)
    filtered = jnp.dot(
        filter_band,
        padded.reshape(time_rows + 2 * HALF, flat_width),
        preferred_element_type=jnp.float32,
    )
    filtered = filtered.astype(jnp.bfloat16)
    contract = (((1,), (1,)), ((), ()))
    flat_test = test_matrix.reshape(rank_total, flat_width)
    partial_sketch = lax.dot_general(
        flat_test, filtered, contract, preferred_element_type=jnp.float32
    )
    orth_basis = orthonormal(partial_sketch)
    for iteration in range(ITERS):
        basis_half = orth_basis.astype(jnp.bfloat16)
        chosen = lax.slice_in_dim(basis_half, 0, rank_rows * lax.axis_size("tm"), axis=0)
        loading_rows = lax.psum_scatter(
            jnp.dot(chosen, filtered, preferred_element_type=jnp.float32),
            "tm",
            scatter_dimension=0,
            tiled=True,
        )
        gathered = lax.all_gather(loading_rows.astype(jnp.bfloat16), "tm", axis=0, tiled=True)
        partial_sketch = lax.dot_general(
            gathered, filtered, contract, preferred_element_type=jnp.float32
        )
        orth_basis = orthonormal(partial_sketch)
    final_half = orth_basis.astype(jnp.bfloat16)
    loadings = lax.psum(jnp.dot(final_half, filtered, preferred_element_type=jnp.float32), "tm")
    captured = jnp.sum(loadings * loadings, axis=0)
    energy = (captured / total_times).reshape(field_count, columns)
    pcs = orth_basis * math.sqrt(total_times)
    return (pcs, energy)


def solution(mesh):
    return jax.shard_map(
        body,
        mesh=mesh,
        in_specs=(P("tm", None, "space"), P(None, None, "space")),
        out_specs=(P(None, "tm"), P(None, "space")),
        check_vma=False,
    )
```

profile of v0, /device:TPU:6, one launch (start us, length us, event | category | flops | bytes accessed | tf_op | source)
XLA Modules:
  0.0 1971.5 jit_solution(5143835336280217606)
XLA Ops:
  7.2 1.9 fusion.24
  9.1 4.3 collective-permute-start
  13.5 1.3 collective-permute-start.1
  14.8 19.1 collective-permute-done
  33.9 4.8 collective-permute-done.1
  38.6 2.6 pad_maximum_fusion
  41.3 6.5 copy.19
  47.8 3.8 convolution_convert_fusion
  51.5 1.2 convolution_bitcast_fusion
  52.8 1.3 dynamic-slice
  54.0 70.0 %all-reduce.9.cloned.1.call-done = f32[64,256]{1,0:T(8,128)} async-done(((f32[64,256]{1,0:T(8,128)}), f32[64,256]{1,0:T(8,128)}) %all-reduce.9.cloned.1.call-update) | async-done | bytes 65552 | tf_op jit(solution)/shard_map/psum | solution.py:47
  124.0 1.1 fusion.25
  125.1 280.1 %psum.50 = f32[64,64]{0,1:T(8,128)S(1)} all-reduce(f32[64,64]{0,1:T(8,128)S(1)} %fusion.25), channel_id=1, replica_groups=mesh['tm'=64,'space'=8] {'tm'}, use_global_device_ids=true, to_apply=%region_1.0 | all-reduce | flops 4096 | bytes 32768 | tf_op jit(solution)/shard_map/psum | solution.py:49
  405.4 5.8 cholesky.59
  411.3 0.6 compare_reduce_fusion.2
  411.9 0.7 fusion.6
  412.6 4.9 custom-call.7
  417.5 1.1 convolution_convert_fusion.2
  418.6 0.8 fusion.26
  419.4 287.3 %all-reduce.16 = bf16[64,4608]{1,0:T(8,128)(2,1)} all-reduce(f32[64,4608]{1,0:T(8,128)S(1)} %fusion.26), channel_id=2, replica_groups=mesh['tm'=64,'space'=8] {'tm'}, use_global_device_ids=true, to_apply=%region_4.0.clone | all-reduce | flops 294912 | bytes 1769472
  706.6 1.5 fusion.23
  708.1 46.9 %all-gather = bf16[64,1,4608]{2,1,0:T(2,128)(2,1)S(1)} all-gather(bf16[1,1,4608]{2,1,0:T(2,128)(2,1)S(1)} %fusion.23), channel_id=1, replica_groups=mesh['tm'=64,'space'=8] {'tm'}, dimensions={0}, use_global_device_ids=true | all-gather | bytes 599040 | tf_op jit(solution)/shard_map/all_gather | solution.py:83
  755.0 1.1 fusion.3
  756.2 62.8 %all-reduce.11.cloned.1.call-done = f32[64,256]{1,0:T(8,128)} async-done(((f32[64,256]{1,0:T(8,128)}), f32[64,256]{1,0:T(8,128)}) %all-reduce.11.cloned.1.call-update) | async-done | bytes 65552 | tf_op jit(solution)/shard_map/psum | solution.py:47
  819.0 1.1 fusion.27
  820.1 280.1 %psum.52 = f32[64,64]{0,1:T(8,128)S(1)} all-reduce(f32[64,64]{0,1:T(8,128)S(1)} %fusion.27), channel_id=1, replica_groups=mesh['tm'=64,'space'=8] {'tm'}, use_global_device_ids=true, to_apply=%region_6.0 | all-reduce | flops 4096 | bytes 32768 | tf_op jit(solution)/shard_map/psum | solution.py:49
  1100.3 5.8 cholesky.70
  1106.2 0.6 compare_reduce_fusion.1
  1106.9 0.7 fusion.7
  1107.5 4.9 custom-call.8
  1112.4 1.1 convolution_convert_fusion.1
  1113.5 0.8 fusion.28
  1114.4 287.2 %all-reduce.17 = bf16[64,4608]{1,0:T(8,128)(2,1)} all-reduce(f32[64,4608]{1,0:T(8,128)S(1)} %fusion.28), channel_id=3, replica_groups=mesh['tm'=64,'space'=8] {'tm'}, use_global_device_ids=true, to_apply=%region_7.0.clone | all-reduce | flops 294912 | bytes 1769472
  1401.5 1.5 fusion.22
  1403.0 47.1 %all-gather.1 = bf16[64,1,4608]{2,1,0:T(2,128)(2,1)S(1)} all-gather(bf16[1,1,4608]{2,1,0:T(2,128)(2,1)S(1)} %fusion.22), channel_id=1, replica_groups=mesh['tm'=64,'space'=8] {'tm'}, dimensions={0}, use_global_device_ids=true | all-gather | bytes 599040 | tf_op jit(solution)/shard_map/all_gather | solution.py:83
  1450.1 1.1 fusion
  1451.3 62.8 %all-reduce.13.cloned.1.call-done = f32[64,256]{1,0:T(8,128)} async-done(((f32[64,256]{1,0:T(8,128)}), f32[64,256]{1,0:T(8,128)}) %all-reduce.13.cloned.1.call-update) | async-done | bytes 65552 | tf_op jit(solution)/shard_map/psum | solution.py:47
  1514.1 1.1 fusion.29
  1515.2 280.1 %psum.54 = f32[64,64]{0,1:T(8,128)S(1)} all-reduce(f32[64,64]{0,1:T(8,128)S(1)} %fusion.29), channel_id=1, replica_groups=mesh['tm'=64,'space'=8] {'tm'}, use_global_device_ids=true, to_apply=%region_9.0 | all-reduce | flops 4096 | bytes 32768 | tf_op jit(solution)/shard_map/psum | solution.py:49
  1795.5 5.8 cholesky.81
  1801.4 0.6 compare_reduce_fusion
  1802.0 0.7 fusion.8
  1802.7 4.9 custom-call.9
  1807.6 1.7 broadcast_multiply_fusion
  1809.3 1.9 fusion.20
  1811.2 151.8 %all-reduce.15.cloned.1.call-done = f32[64,4608]{1,0:T(8,128)} async-done(((f32[64,4608]{1,0:T(8,128)}), f32[64,4608]{1,0:T(8,128)}) %all-reduce.15.cloned.1.call-update) | async-done | bytes 1179664 | tf_op jit(solution)/shard_map/psum | solution.py:89
  1963.0 1.4 multiply_reduce_fusion
  1964.4 0.6 div.16
  (25 shorter events, 0.6 us)
Async XLA Ops:
  7.2 31.5 %copy-start = (bf16[256,3,1536]{2,0,1:T(8,128)(2,1)S(1)}, bf16[256,3,1536]{2,0,1:T(8,128)(2,1)}, u32[]{:S(2)}) copy-start(bf16[256,3,1536]{2,0,1:T(8,128)(2,1)} %param.6) | copy-start | bytes 7077892
  7.2 7.6 copy-start.1
  7.2 116.8 %all-reduce.9.cloned.1.call-start = ((), (), s32[]{:S(2)}) async-start(), calls=%async_computation | async-start | bytes 131072 | tf_op jit(solution)/shard_map/psum | solution.py:47
  9.1 24.8 %collective-permute-start = (bf16[100,3,1536]{2,0,1:T(8,128)(2,1)S(1)}, bf16[100,3,1536]{2,0,1:T(8,128)(2,1)S(1)}, u32[]{:S(2)}, u32[]{:S(2)}) collective-permute-start(bf16[100,3,1536]{2,0,1:T(8,128)(2,1)S(1)} %get-tuple-element.4), channel_id=1, source_target_pairs={{0,8},{8,16},{16,24},{24,32},{32,40},{40,48},{48,56},{56,64},{64,7... | collective-permute-start | bytes 2764808 | tf_op jit(solution)/shard_map/ppermute | solution.py:24
  13.5 25.2 %collective-permute-start.1 = (bf16[100,3,1536]{2,0,1:T(8,128)(2,1)S(1)}, bf16[100,3,1536]{2,0,1:T(8,128)(2,1)S(1)}, u32[]{:S(2)}, u32[]{:S(2)}) collective-permute-start(bf16[100,3,1536]{2,0,1:T(8,128)(2,1)S(1)} %get-tuple-element.5), channel_id=1, source_target_pairs={{8,0},{16,8},{24,16},{32,24},{40,32},{48,40},{56,48},{64,56},{72,6... | collective-permute-start | bytes 2764808 | tf_op jit(solution)/shard_map/ppermute | solution.py:25
  41.2 6.5 copy-start.2
  52.7 766.3 %all-reduce.11.cloned.1.call-start = ((), (), s32[]{:S(2)}) async-start(), calls=%async_computation.1 | async-start | bytes 131072 | tf_op jit(solution)/shard_map/psum | solution.py:47
  756.2 757.9 %all-reduce.13.cloned.1.call-start = ((), (), s32[]{:S(2)}) async-start(), calls=%async_computation.2 | async-start | bytes 131072 | tf_op jit(solution)/shard_map/psum | solution.py:47
  1451.2 511.7 %all-reduce.15.cloned.1.call-start = ((), (), s32[]{:S(2)}) async-start(), calls=%async_computation.3 | async-start | bytes 2359296 | tf_op jit(solution)/shard_map/psum | solution.py:89
Sparse Core Ops, SparseCore 0:
  52.8 71.1 all-reduce.8
  756.3 62.6 all-reduce.10
  1451.4 62.7 all-reduce.12
  1811.3 151.6 all-reduce.14
where the time goes:
time: 1970 us
  blocking collectives  1510 us (77%)
  waiting for transfers between devices  371 us (19%)
  other arithmetic  40.2 us (2%)
    psum x3, blocking collectives, orthonormal(): gram_total = lax.psum(gram_local, 'tm')  840 us
    unnamed x2, blocking collectives  574 us
    psum x3, waiting for transfers between devices, orthonormal(): sketch = lax.psum(partial_sketch, 'space')  196 us
    psum x1, waiting for transfers between devices, body(): lax.psum(jnp.dot(final_half, filtered, preferred_element_type=jnp.float32...  152 us
    all_gather x2, blocking collectives, body(): lax.all_gather(loading_rows.astype(jnp.bfloat16), 'tm', axis=0, tiled=True)  94 us
  transfers between devices with their start and end apart: 6, of which 6 were waited for; matrix products, arithmetic and copies ran while one was open for 0% of the time, Pallas kernels for 0%

commit v1 on v0

v1 whole, which is shorter than its diff:
```python
import functools
import math

import jax
import jax.numpy as jnp
import numpy as np
from jax import lax
from jax.experimental import pallas as pl
from jax.experimental.pallas import tpu as pltpu
from jax.sharding import PartitionSpec as P

MESH = pl.DeviceIdType.MESH
HALF = 100
ITERS = 2
PAD = 128
low_cutoff = 1.0 / 96.0
high_cutoff = 1.0 / 24.0

SIDE = 8
PARTS = 8
K = 64
ROWS = 256
WIDE = 4608
PACK = WIDE // 2
HALFROWS = PACK // 2
CHUNK = HALFROWS // SIDE
MAIN = 16
LEFT = MAIN * SIDE
F32, BF16 = jnp.float32, jnp.bfloat16
HI = lax.Precision.HIGHEST
NT = (((1,), (1,)), ((), ()))
TN = (((0,), (0,)), ((), ()))
ORDER = (4, 3, 5, 2, 6, 1, 7)


def lanczos(half_width):
    lag = np.arange(-half_width, half_width + 1) * 1.0
    safe = np.where(lag == 0, 1.0, lag)
    response = (np.sin(2 * np.pi * high_cutoff * safe) - np.sin(2 * np.pi * low_cutoff * safe)) / (np.pi * safe)
    response = np.where(lag == 0, 2.0 * (high_cutoff - low_cutoff), response)
    ratio = np.pi * safe / (half_width + 1)
    sigma = np.where(lag == 0, 1.0, np.sin(ratio) / ratio)
    return (response * sigma).astype(np.float32)


def band_matrix():
    lag = np.arange(3 * ROWS)[:, None] - np.arange(ROWS + 2 * PAD)[None, :] - (ROWS - PAD)
    taps = lanczos(HALF)[np.clip(lag + HALF, 0, 2 * HALF)]
    return np.where(np.abs(lag) <= HALF, taps, 0.0).astype(np.float32)


def split3(x):
    hi = x.astype(BF16)
    rest = x - hi.astype(F32)
    mid = rest.astype(BF16)
    low = (rest - mid.astype(F32)).astype(BF16)
    return jnp.concatenate([hi, mid, low], axis=0)


def filter_rows(x, band):
    out = jnp.dot(split3(x), band, preferred_element_type=F32)
    return out[0:K] + out[K : 2 * K] + out[2 * K : 3 * K]


def factor(gram):
    row_id = lax.broadcasted_iota(jnp.int32, (K, 2 * K), 0)
    lane_id = lax.broadcasted_iota(jnp.int32, (K, 2 * K), 1)
    a = jnp.where(lane_id < K, gram, 0.0) + jnp.where(lane_id == row_id + K, 1.0, 0.0)
    blocks = [a[8 * b : 8 * b + 8] for b in range(K // 8)]
    sub_id = lax.broadcasted_iota(jnp.int32, (8, 2 * K), 0)
    for j in range(K):
        b, r = divmod(j, 8)
        inv = lax.rsqrt(blocks[b][r : r + 1, j : j + 1])
        row = blocks[b][r : r + 1, :] * inv
        scaled = row * inv
        for c in range(b, K // 8):
            col = blocks[c][:, j : j + 1]
            nxt = blocks[c] - col * scaled
            if c == b:
                nxt = jnp.where(sub_id > r, nxt, jnp.where(sub_id == r, row, blocks[c]))
            blocks[c] = nxt
    return jnp.concatenate(blocks, axis=0)


def kernel(
    x_hbm, t_hbm, band_ref, pcs_ref, eb,
    xv, tv, xt, lbt, rbuf, srr, rext, s2, wt, gzs, gzr, gys, gyr, gfull, v1, r1, v2, r2, res, linv2, racc,
    in_sem,
    sr_s, sr_r, ah_s, ah_r, gz_s, gz_r, gy_s, gy_r, gs_s, gs_r,
    p1_s, p1_r, p2_s, p2_r, a1_s, a1_r, a2_s, a2_r, e1_s, e1_r, e2_s, e2_r,
):
    t, s = lax.axis_index("tm"), lax.axis_index("space")
    y, z = t // SIDE, t % SIDE
    times = SIDE * SIDE

    def at_z(p):
        return (y * SIDE + p, s)

    def at_y(p):
        return (p * SIDE + z, s)

    first = ((z, at_z), (y, at_y))
    second = ((y, at_y), (z, at_z))
    t_next, t_prev = (t + 1) % times, (t + times - 1) % times

    loads = []
    for f in range(3):
        cols = pl.ds(f * (WIDE // 3), WIDE // 3)
        loads.append(pltpu.make_async_copy(x_hbm.at[f], xv.at[:, cols], in_sem.at[f]))
        loads.append(pltpu.make_async_copy(t_hbm.at[f], tv.at[:, cols], in_sem.at[3 + f]))
    for c in loads:
        c.start()

    barrier = pltpu.get_barrier_semaphore()
    greet = []
    for d in range(1, SIDE):
        greet += [at_z((z + d) % SIDE), at_y((y + d) % SIDE), (t, (s + d) % PARTS)]
    for d in range(PARTS):
        greet += [(t_next, (s + d) % PARTS), (t_prev, (s + d) % PARTS)]
    for dev in greet:
        pl.semaphore_signal(barrier, inc=1, device_id=dev, device_id_type=MESH)

    s2[pl.ds(K, K), :] = jnp.zeros((K, ROWS), F32)
    wt[...] = jnp.zeros((4 * K, 2 * ROWS), BF16)
    for c in loads:
        c.wait()
    rbuf[...] = lax.dot_general(tv[...], xv[...], NT, preferred_element_type=F32)
    pl.semaphore_wait(barrier, len(greet))

    def copy(src, dst, send, recv, dev):
        return pltpu.make_async_remote_copy(
            src_ref=src, dst_ref=dst, send_sem=send, recv_sem=recv, device_id=dev, device_id_type=MESH
        )

    my_rows = pl.ds(pl.multiple_of(s * 8, 8), 8)

    def iteration(i, carry):
        sends = []
        for d in range(1, PARTS):
            p = (s + d) % PARTS
            c = copy(rbuf.at[pl.ds(pl.multiple_of(p * 8, 8), 8)], srr.at[d - 1], sr_s.at[d - 1], sr_r.at[d - 1], (t, p))
            c.start()
            sends.append(c)

        @pl.when(i == 0)
        def _():
            for j in range(PACK // 128):
                for side in range(2):
                    xt[pl.ds(j * 128, 128), pl.ds(side * ROWS, ROWS)] = xv[:, pl.ds(side * PACK + j * 128, 128)].T

        total = rbuf[my_rows, :]
        for d in range(1, PARTS):
            sends[d - 1].wait_recv()
            total = total + srr[d - 1]
        rext[my_rows, pl.ds(ROWS, ROWS)] = total

        gath = []
        mine = rext.at[my_rows, pl.ds(ROWS, ROWS)]
        n = 0
        for d in range(PARTS):
            p = (s + d) % PARTS
            for tt, lane in ((t_next, 0), (t_prev, 2 * ROWS), (t, ROWS)):
                if d == 0 and lane == ROWS:
                    continue
                c = copy(mine, rext.at[my_rows, pl.ds(lane, ROWS)], ah_s.at[n], ah_r.at[n], (tt, p))
                c.start()
                gath.append(c)
                n += 1
        for c in gath:
            c.wait_recv()
        for c in sends + gath:
            c.wait_send()

        hour = lax.broadcasted_iota(jnp.int32, (1, ROWS + 2 * PAD), 1) + (t * ROWS - PAD)
        inside = jnp.logical_and(hour >= 0, hour < times * ROWS)
        r_in = rext[...]
        slab = lax.broadcasted_iota(jnp.int32, (1, 3 * ROWS), 1) + (t - 1) * ROWS
        r_in = jnp.where(jnp.logical_and(slab >= 0, slab < times * ROWS), r_in, 0.0)
        s_ext = filter_rows(r_in, band_ref[...])
        s_ext = jnp.where(inside, s_ext, 0.0)
        s2[pl.ds(0, K), :] = s_ext[:, PAD : PAD + ROWS]
        gzs[...] = lax.dot_general(s2[my_rows, :], s2[...], NT, precision=HI, preferred_element_type=F32)
        gz = []
        for d in range(1, SIDE):
            c = copy(gzs, gzr.at[d - 1], gz_s.at[d - 1], gz_r.at[d - 1], at_z((z + d) % SIDE))
            c.start()
            gz.append(c)
        u = filter_rows(s_ext, band_ref[pl.ds(0, ROWS + 2 * PAD), pl.ds(0, ROWS)])
        u_hi = u.astype(BF16)
        u_mid = (u - u_hi.astype(F32)).astype(BF16)
        wt[pl.ds(0, K), pl.ds(0, ROWS)] = u_hi
        wt[pl.ds(K, K), pl.ds(ROWS, ROWS)] = u_hi
        wt[pl.ds(2 * K, K), pl.ds(0, ROWS)] = u_mid
        wt[pl.ds(3 * K, K), pl.ds(ROWS, ROWS)] = u_mid

        def product(h, p):
            rows = pl.ds(pl.multiple_of(h * HALFROWS + p * CHUNK, 16), CHUNK)
            out = lax.dot_general(xt[rows, :], wt[...], NT, preferred_element_type=F32)
            return out[:, 0:128] + out[:, 128:256]

        one = []
        for d in ORDER:
            for h in range(2):
                pos, dev = first[h]
                p = (pos + d) % SIDE
                v1[h, d] = product(h, p)
                c = copy(v1.at[h, d], r1.at[h, d - 1], p1_s.at[h, d - 1], p1_r.at[h, d - 1], dev(p))
                c.start()
                one.append((c, h, d))
        for h in range(2):
            v1[h, 0] = product(h, first[h][0])

        total = gzs[...]
        for d in range(1, SIDE):
            gz[d - 1].wait_recv()
            total = total + gzr[d - 1]
        gys[...] = total
        gy = []
        for d in range(1, SIDE):
            c = copy(gys, gyr.at[d - 1], gy_s.at[d - 1], gy_r.at[d - 1], at_y((y + d) % SIDE))
            c.start()
            gy.append(c)
        total = gys[...]
        for d in range(1, SIDE):
            gy[d - 1].wait_recv()
            total = total + gyr[d - 1]
        gfull[my_rows, :] = total
        gs = []
        for d in range(1, PARTS):
            c = copy(gfull.at[my_rows], gfull.at[my_rows], gs_s.at[d - 1], gs_r.at[d - 1], (t, (s + d) % PARTS))
            c.start()
            gs.append(c)

        for c, h, d in one:
            c.wait_recv()
        two = []
        for h in range(2):
            total = v1[h, 0]
            for d in range(1, SIDE):
                total = total + r1[h, d - 1]
            for q in range(SIDE):
                v2[h, q, pl.ds(0, MAIN)] = total[q * MAIN : (q + 1) * MAIN]
                v2[h, q, pl.ds(MAIN, MAIN)] = total[LEFT:CHUNK]
            pos, dev = second[h]
            for d in range(1, SIDE):
                q = (pos + d) % SIDE
                c = copy(v2.at[h, q], r2.at[h, d - 1], p2_s.at[h, d - 1], p2_r.at[h, d - 1], dev(q))
                c.start()
                two.append(c)

        for c in gs:
            c.wait_recv()
        aug = factor(gfull[...])
        lane_id = lax.broadcasted_iota(jnp.int32, (K, 2 * K), 1)
        low = jnp.where(lane_id >= K, aug, 0.0)
        linv2[pl.ds(0, K), :] = pltpu.roll(low, K, 1)
        linv2[pl.ds(K, K), :] = low

        for c in two:
            c.wait_recv()
        for h in range(2):
            total = v2[h, second[h][0]]
            for d in range(1, SIDE):
                total = total + r2[h, d - 1]
            res[pl.ds(2 * MAIN * h, 2 * MAIN), :] = total
        res[...] = lax.dot_general(res[...], linv2[...], NT, precision=HI, preferred_element_type=F32)
        for c in gz + gy + gs + two:
            c.wait_send()
        for c, h, d in one:
            c.wait_send()

        @pl.when(i < ITERS)
        def _():
            gat = []
            for h in range(2):
                base = h * HALFROWS + first[h][0] * CHUNK
                pos, dev = second[h]
                own = pl.ds(pl.multiple_of(base + pos * MAIN, MAIN), MAIN)
                lbt[own, :] = res[pl.ds(2 * MAIN * h, MAIN), :].astype(BF16)
                lbt[pl.ds(pl.multiple_of(base + LEFT, MAIN), MAIN), :] = res[pl.ds(2 * MAIN * h + MAIN, MAIN), :].astype(BF16)
                for d in ORDER:
                    c = copy(lbt.at[own], lbt.at[own], a1_s.at[h, d - 1], a1_r.at[h, d - 1], dev((pos + d) % SIDE))
                    c.start()
                    gat.append((c, h))
            out = []
            for h in range(2):
                for c, hh in gat:
                    if hh == h:
                        c.wait_recv()
                pos, dev = first[h]
                own = pl.ds(pl.multiple_of(h * HALFROWS + pos * CHUNK, 16), CHUNK)
                for d in ORDER:
                    c = copy(lbt.at[own], lbt.at[own], a2_s.at[h, d - 1], a2_r.at[h, d - 1], dev((pos + d) % SIDE))
                    c.start()
                    out.append(c)
            for c in out:
                c.wait_recv()
            prod = lax.dot_general(lbt[...], xt[...], TN, preferred_element_type=F32)
            rbuf[...] = prod[0:K, 0:ROWS] + prod[K : 2 * K, ROWS : 2 * ROWS]
            for c, h in gat:
                c.wait_send()
            for c in out:
                c.wait_send()

        return carry

    lax.fori_loop(0, ITERS + 1, iteration, 0)

    pcs_ref[...] = jnp.dot(linv2[pl.ds(0, K), :], s2[...], precision=HI, preferred_element_type=F32)
    square = res[...] * res[...]
    lane_id = lax.broadcasted_iota(jnp.int32, (K, 2 * K), 1)
    stack = jnp.concatenate([jnp.where(lane_id < K, square, 0.0), jnp.where(lane_id >= K, square, 0.0)], axis=0)
    sums = lax.dot_general(jnp.ones((8, 2 * K), F32), stack, NT, precision=HI, preferred_element_type=F32)
    own = z * SIDE + y
    eb[own] = sums[0:1, :]
    e1 = []
    for d in range(1, SIDE):
        c = copy(eb.at[own], eb.at[own], e1_s.at[d - 1], e1_r.at[d - 1], at_y((y + d) % SIDE))
        c.start()
        e1.append(c)
    for c in e1:
        c.wait_recv()
    e2 = []
    group = pl.ds(z * SIDE, SIDE)
    for d in range(1, SIDE):
        c = copy(eb.at[group], eb.at[group], e2_s.at[d - 1], e2_r.at[d - 1], at_z((z + d) % SIDE))
        c.start()
        e2.append(c)
    for c in e2:
        c.wait_recv()
    for c in e1 + e2:
        c.wait_send()


def body(fields, test_matrix):
    x = jnp.transpose(fields, (1, 0, 2))
    tm = jnp.transpose(test_matrix, (1, 0, 2))
    band = jnp.asarray(band_matrix()).astype(BF16)
    vm = pltpu.VMEM
    dma = pltpu.SemaphoreType.DMA
    seven, halves = (SIDE - 1,), (2, SIDE - 1)
    scratch = [
        vm((ROWS, WIDE), BF16), vm((K, WIDE), BF16), vm((PACK, 2 * ROWS), BF16), vm((PACK, 2 * K), BF16),
        vm((K, ROWS), F32), vm((PARTS - 1, 8, ROWS), F32), vm((K, 3 * ROWS), F32), vm((2 * K, ROWS), F32),
        vm((4 * K, 2 * ROWS), BF16),
        vm((8, 2 * K), F32), vm((SIDE - 1, 8, 2 * K), F32), vm((8, 2 * K), F32), vm((SIDE - 1, 8, 2 * K), F32), vm((K, 2 * K), F32),
        vm((2, SIDE, CHUNK, 128), F32), vm((2, SIDE - 1, CHUNK, 128), F32),
        vm((2, SIDE, 2 * MAIN, 128), F32), vm((2, SIDE - 1, 2 * MAIN, 128), F32),
        vm((K, 128), F32), vm((2 * K, 2 * K), F32), vm((8, 128), F32),
        dma((6,)),
        dma(seven), dma(seven), dma((3 * PARTS - 1,)), dma((3 * PARTS - 1,)),
        dma(seven), dma(seven), dma(seven), dma(seven), dma(seven), dma(seven),
        dma(halves), dma(halves), dma(halves), dma(halves), dma(halves), dma(halves), dma(halves), dma(halves),
        dma(seven), dma(seven), dma(seven), dma(seven),
    ]
    basis, parts = pl.pallas_call(
        kernel,
        out_shape=(
            jax.ShapeDtypeStruct((K, ROWS), F32),
            jax.ShapeDtypeStruct((SIDE * SIDE, 1, 128), F32),
        ),
        in_specs=[
            pl.BlockSpec(memory_space=pl.ANY),
            pl.BlockSpec(memory_space=pl.ANY),
            pl.BlockSpec(memory_space=pltpu.VMEM),
        ],
        out_specs=(pl.BlockSpec(memory_space=pltpu.VMEM), pl.BlockSpec(memory_space=pltpu.VMEM)),
        scratch_shapes=scratch,
        compiler_params=pltpu.CompilerParams(collective_id=0, has_side_effects=True, vmem_limit_bytes=48 << 20),
    )(x, tm, band)
    total_times = SIDE * SIDE * ROWS
    pcs = basis * math.sqrt(total_times)
    e = parts.reshape(SIDE, SIDE, 2, 2, 2, MAIN)
    main0 = jnp.transpose(e[:, :, :, 0, 0], (2, 0, 1, 3)).reshape(2, SIDE, LEFT)
    last0 = jnp.transpose(e[:, 0, :, 0, 1], (1, 0, 2))
    main1 = jnp.transpose(e[:, :, :, 1, 0], (2, 1, 0, 3)).reshape(2, SIDE, LEFT)
    last1 = jnp.transpose(e[0, :, :, 1, 1], (1, 0, 2))
    half0 = jnp.concatenate([main0, last0], axis=2).reshape(2, HALFROWS)
    half1 = jnp.concatenate([main1, last1], axis=2).reshape(2, HALFROWS)
    energy = jnp.concatenate([half0, half1], axis=1).reshape(3, WIDE // 3) / total_times
    return (pcs, energy)


def solution(mesh):
    return jax.shard_map(
        body,
        mesh=mesh,
        in_specs=(P("tm", None, "space"), P(None, None, "space")),
        out_specs=(P(None, "tm"), P(None, "space")),
        check_vma=False,
    )
```

time: 1970 us -> 172 us (0.09)
  blocking collectives: 1510 us -> 0 us
  waiting for transfers between devices: 371 us -> 0 us
  Pallas kernels: 0 us -> 163 us
  other arithmetic: 40.2 us -> 1.38 us
    psum x3 -> x0, blocking collectives: 840 us -> none  [orthonormal(): gram_total = lax.psum(gram_local, 'tm')]
    unnamed x2 -> x0, blocking collectives: 574 us -> none
    psum x4 -> x0, waiting for transfers between devices: 347 us -> none  [the longest x3 196 us: orthonormal(): sketch = lax.psum(partial_sketch, 'space')]
    pallas_call x0 -> x1, Pallas kernels: none -> 163 us  [body(): pl.pallas_call(kernel, out_shape=(jax.ShapeDtypeStruct((K, ROWS), F32), j...]
    all_gather x2 -> x0, blocking collectives: 94 us -> none  [body(): lax.all_gather(loading_rows.astype(jnp.bfloat16), 'tm', axis=0, tiled=True)]
    another operation x15 -> x0, other arithmetic: 36.2 us -> none  [the longest x9 19.6 us: orthonormal(): lower_factor = jnp.linalg.cholesky(gram_total)]
    ppermute x2 -> x0, waiting for transfers between devices: 23.8 us -> none  [the longest x1 19.1 us: with_halo(): before = lax.ppermute(last, axis, up)]
  transfers between devices with their start and end apart: 6 -> 0, of which waited for: 6 -> 0; matrix products, arithmetic and copies ran while one was open for 0% -> 0% of each run, Pallas kernels for 0% -> 0%
where the time goes in v1:
time: 172 us; the launch traced here: 171 us
  Pallas kernels  163 us (95%)
  local copies, waits for them, and re-layouts  5.86 us (3%)
    pallas_call x1, Pallas kernels, body(): pl.pallas_call(kernel, out_shape=(jax.ShapeDtypeStruct((K, ROWS), F32), j...  163 us
    unnamed x10, local copies, waits for them, and re-layouts  3.89 us

profile of v1, /device:TPU:6, one launch (start us, length us, event | category | flops | bytes accessed | tf_op | source)
XLA Modules:
  0.0 171.4 jit_solution(2246356721817981655)
XLA Ops:
  0.6 0.0 copy-start
  0.6 1.7 copy-done
  2.3 0.0 copy-start.1
  2.3 1.1 copy-done.1
  3.4 0.0 copy-start.2
  3.4 1.1 copy-done.2
  4.5 163.4 %shard_map.50 = (f32[64,256]{1,0:T(8,128)S(1)}, f32[64,1,128]{2,1,0:T(1,128)S(1)}) custom-call(bf16[3,256,1536]{2,1,0:T(8,128)(2,1)S(1)} %bitcast.26, bf16[3,64,1536]{2,1,0:T(8,128)(2,1)S(1)} %bitcast.27, bf16[768,512]{1,0:T(8,128)(2,1)S(1)} %copy-done.1), custom_call_target="tpu_custom_call" | custom-call | tf_op jit(solution)/shard_map/pallas_call | solution.py:356
  167.9 0.6 broadcast_multiply_fusion
  168.5 0.5 broadcast.6
  169.0 0.7 reduce.3
  169.7 0.4 reshape.22
  170.2 0.1 fusion
  170.3 0.1 reshape.23
  170.4 0.1 reshape.24
  170.5 0.1 reshape.25
  170.6 0.1 reshape.26
  170.7 0.6 div.10
  (9 shorter events, 0.1 us)
Async XLA Ops:
  0.6 1.7 copy-start
  2.3 1.1 copy-start.1
  3.4 1.1 copy-start.2
